TPU v7x, 32 devices: a whole 2x2x4 slice. The times are simulated.
32 devices in a mesh: rep: 2 (over x), grp: 16 (over z, y, core).
Axes of the slice: x: 2, y: 2, z: 4, core: 2. Of those that a mesh axis runs over, the one named last changes fastest.
Arguments:
- images: bfloat16 [3, 32, 197, 768], P(None, ('rep', 'grp')), may hold values from -6 to 6
- attn_qkv: bfloat16 [768, 2304], P('grp'), may hold values from -0.21875 to 0.21875
- attn_proj: bfloat16 [768, 768], P('grp'), may hold values from -1.25 to 1.25
- router: bfloat16 [768, 16], P('grp'), may hold values from -0.15625 to 0.15625
- gain_attn: bfloat16 [768], P('grp'), may hold values from 0.5 to 1.5
- gain_moe: bfloat16 [768], P('grp'), may hold values from 0.5 to 1.5
- expert_in: bfloat16 [16, 768, 3072], P('grp'), may hold values from -0.21875 to 0.21875
- expert_out: bfloat16 [16, 3072, 768], P('grp'), may hold values from -1.25 to 1.25
- routes: int32 [3, 32, 197, 2], P(None, ('rep', 'grp')), may hold values from 0 to 15, all different within a row
- cotangent: bfloat16 [3, 32, 197, 768], P(None, ('rep', 'grp')), may hold values from -6 to 6
Outputs:
- output: bfloat16 [3, 32, 197, 768], P(None, ('rep', 'grp'))
- grad_images: bfloat16 [3, 32, 197, 768], P(None, ('rep', 'grp'))
- grad_qkv: float32 [768, 2304], P('grp')
- grad_proj: float32 [768, 768], P('grp')
- grad_router: float32 [768, 16], P('grp')
- grad_gain_attn: float32 [768], P('grp')
- grad_gain_moe: float32 [768], P('grp')
- grad_expert_in: float32 [16, 768, 3072], P('grp')
- grad_expert_out: float32 [16, 3072, 768], P('grp')
Inputs may be any that keep to these rules, and one draw needn't show every extreme that they name: Each token's two routes name two different experts.
All inputs are finite; a program needn't handle non-finite values.
Results may differ from a plain program's by a relative error of at most 0.023.
Values may be sent and summed in bfloat16 or wider, within the bound.
No kernel may reach another device: no remote copies, remote signals or barrier semaphores. Data moves between devices by JAX's collectives and lax.ppermute only.
A program may use at most 192 MiB of HBM per device.

v0:
```python
import jax
import jax.numpy as jnp
from jax import lax
from jax.sharding import PartitionSpec as P

HEADS = 12
SEQ = 197


EPSILON = 1e-06


def contract_first(left, right):
    return lax.dot_general(
        left, right, (((0,), (0,)), ((), ())), preferred_element_type=jnp.float32
    )


def contract_last(left, right):
    return lax.dot_general(
        left, right, (((1,), (1,)), ((), ())), preferred_element_type=jnp.float32
    )


def matmul(left, right):
    return jnp.dot(left, right, preferred_element_type=jnp.float32)


def normalize(values, gain_vector):
    center = values - jnp.mean(values, -1, keepdims=True)
    inverse = lax.rsqrt(jnp.mean(center * center, -1, keepdims=True) + EPSILON)
    unit_rows = center * inverse
    return (unit_rows, inverse, unit_rows * gain_vector.astype(jnp.float32))


def norm_backward(grad_rows, unit_rows, inverse, gain_vector):
    scaled = grad_rows * gain_vector.astype(jnp.float32)
    inner = (
        scaled
        - jnp.mean(scaled, -1, keepdims=True)
        - unit_rows * jnp.mean(scaled * unit_rows, -1, keepdims=True)
    )
    return (inner * inverse, jnp.sum(grad_rows * unit_rows, 0))


def split_heads(packed):
    images_count = packed.shape[0] // SEQ
    head_dim = packed.shape[1] // (3 * HEADS)
    pieces = packed.reshape(images_count, SEQ, 3, HEADS, head_dim)
    return (pieces[:, :, 0], pieces[:, :, 1], pieces[:, :, 2], head_dim ** (-0.5))


def attend_forward(packed):
    query, keys, values, factor = split_heads(packed)
    scores = jnp.einsum("ishd,ithd->ihst", query, keys, preferred_element_type=jnp.float32) * factor
    highest = jnp.max(scores, -1, keepdims=True)
    log_total = highest + jnp.log(jnp.sum(jnp.exp(scores - highest), -1, keepdims=True))
    weights = jnp.exp(scores - log_total).astype(jnp.bfloat16)
    mixture = jnp.einsum("ihst,ithd->ishd", weights, values, preferred_element_type=jnp.float32)
    return (mixture.reshape(packed.shape[0], -1).astype(jnp.bfloat16), log_total)


def attend_backward(packed, log_total, grad_mixture):
    query, keys, values, factor = split_heads(packed)
    scores = jnp.einsum("ishd,ithd->ihst", query, keys, preferred_element_type=jnp.float32) * factor
    weights = jnp.exp(scores - log_total)
    weights_low = weights.astype(jnp.bfloat16)
    grad_heads = grad_mixture.reshape(query.shape)
    grad_values = jnp.einsum(
        "ihst,ishd->ithd", weights_low, grad_heads, preferred_element_type=jnp.float32
    )
    grad_weights = jnp.einsum(
        "ishd,ithd->ihst", grad_heads, values, preferred_element_type=jnp.float32
    )
    grad_scores = (
        weights * (grad_weights - jnp.sum(grad_weights * weights, -1, keepdims=True))
    ).astype(jnp.bfloat16)
    grad_query = (
        jnp.einsum("ihst,ithd->ishd", grad_scores, keys, preferred_element_type=jnp.float32)
        * factor
    )
    grad_keys = (
        jnp.einsum("ihst,ishd->ithd", grad_scores, query, preferred_element_type=jnp.float32)
        * factor
    )
    stacked = jnp.stack([grad_query, grad_keys, grad_values], 2)
    return stacked.reshape(packed.shape[0], -1).astype(jnp.bfloat16)


def route_table(route_rows, experts, capacity):
    ordering = jnp.concatenate([route_rows[:, 0], route_rows[:, 1]])
    onehot = (ordering[:, None] == jnp.arange(experts, dtype=jnp.int32)).astype(jnp.int32)
    before = jnp.cumsum(onehot, axis=0, dtype=jnp.int32) - onehot
    slot_rank = jnp.sum(before * onehot, axis=-1, dtype=jnp.int32)
    target = jnp.where(slot_rank < capacity, ordering * capacity + slot_rank, -1)
    table = (target[:, None] == jnp.arange(experts * capacity, dtype=jnp.int32)).astype(
        jnp.bfloat16
    )
    return (table, onehot.astype(jnp.float32).reshape(2, route_rows.shape[0], experts))


def shards(
    images,
    attn_qkv,
    attn_proj,
    router,
    gain_attn,
    gain_moe,
    expert_in,
    expert_out,
    routes,
    cotangent,
):
    experts = lax.axis_size("grp")
    micro_count = images.shape[0]
    model_width = images.shape[3]
    rows_count = images.shape[1] * SEQ
    capacity = max(2, 8 * rows_count // (3 * experts))
    weight_in = expert_in[0]
    weight_out = expert_out[0]
    dense_full = (
        jnp.zeros((model_width, attn_qkv.shape[1]), jnp.float32),
        jnp.zeros((model_width, attn_proj.shape[1]), jnp.float32),
        jnp.zeros((model_width, router.shape[1]), jnp.float32),
        jnp.zeros((model_width,), jnp.float32),
        jnp.zeros((model_width,), jnp.float32),
    )
    dense_shard = tuple(
        (
            jnp.zeros(piece.shape, jnp.float32)
            for piece in (attn_qkv, attn_proj, router, gain_attn, gain_moe)
        )
    )
    in_total = jnp.zeros(weight_in.shape, jnp.float32)
    out_total = jnp.zeros(weight_out.shape, jnp.float32)
    outputs = []
    input_grads = []
    for micro_index in range(micro_count):
        gathered = (
            lax.all_gather(attn_qkv, "grp", axis=0, tiled=True),
            lax.all_gather(attn_proj, "grp", axis=0, tiled=True),
            lax.all_gather(router, "grp", axis=0, tiled=True),
            lax.all_gather(gain_attn, "grp", axis=0, tiled=True),
            lax.all_gather(gain_moe, "grp", axis=0, tiled=True),
        )
        full_qkv, full_proj, full_router, full_gain_attn, full_gain_moe = gathered
        states = images[micro_index].reshape(rows_count, model_width).astype(jnp.float32)
        unit_one, inverse_one, scaled_one = normalize(states, full_gain_attn)
        normed_one = scaled_one.astype(jnp.bfloat16)
        packed = matmul(normed_one, full_qkv).astype(jnp.bfloat16)
        mixture, log_total = attend_forward(packed)
        middle = states + matmul(mixture, full_proj)
        unit_two, inverse_two, scaled_two = normalize(middle, full_gain_moe)
        normed_two = scaled_two.astype(jnp.bfloat16)
        probabilities = jax.nn.softmax(matmul(normed_two, full_router), axis=-1)
        table, picked = route_table(routes[micro_index].reshape(rows_count, 2), experts, capacity)
        gate_values = jnp.sum(picked * probabilities[None], -1)
        doubled = jnp.concatenate([normed_two, normed_two], 0)
        outgoing = (
            contract_first(table, doubled)
            .astype(jnp.bfloat16)
            .reshape(experts, capacity, model_width)
        )
        arrived = lax.all_to_all(outgoing, "grp", split_axis=0, concat_axis=0, tiled=True)
        slots_in = arrived.reshape(-1, model_width)
        hidden = matmul(slots_in, weight_in)
        active = jax.nn.gelu(hidden, approximate=False).astype(jnp.bfloat16)
        result = matmul(active, weight_out).astype(jnp.bfloat16)
        returned = lax.all_to_all(
            result.reshape(experts, capacity, model_width),
            "grp",
            split_axis=0,
            concat_axis=0,
            tiled=True,
        )
        per_token = matmul(table, returned.reshape(-1, model_width)).reshape(
            2, rows_count, model_width
        )
        output = middle + (
            gate_values[0][:, None] * per_token[0] + gate_values[1][:, None] * per_token[1]
        )
        outputs.append(output.astype(jnp.bfloat16).reshape(images.shape[1:]))
        gathered = (
            lax.all_gather(attn_qkv, "grp", axis=0, tiled=True),
            lax.all_gather(attn_proj, "grp", axis=0, tiled=True),
            lax.all_gather(router, "grp", axis=0, tiled=True),
            lax.all_gather(gain_attn, "grp", axis=0, tiled=True),
            lax.all_gather(gain_moe, "grp", axis=0, tiled=True),
        )
        full_qkv, full_proj, full_router, full_gain_attn, full_gain_moe = gathered
        grad_y = cotangent[micro_index].reshape(rows_count, model_width).astype(jnp.float32)
        grad_gates = jnp.sum(grad_y[None] * per_token, -1)
        grad_tokens = (
            (gate_values[:, :, None] * grad_y[None])
            .reshape(2 * rows_count, model_width)
            .astype(jnp.bfloat16)
        )
        grad_slots = (
            contract_first(table, grad_tokens)
            .astype(jnp.bfloat16)
            .reshape(experts, capacity, model_width)
        )
        grad_result = lax.all_to_all(
            grad_slots, "grp", split_axis=0, concat_axis=0, tiled=True
        ).reshape(-1, model_width)
        grad_active = contract_last(grad_result, weight_out)
        out_total = out_total + contract_first(active, grad_result)
        unused, gelu_pull = jax.vjp(lambda values: jax.nn.gelu(values, approximate=False), hidden)
        grad_hidden = gelu_pull(grad_active)[0].astype(jnp.bfloat16)
        in_total = in_total + contract_first(slots_in, grad_hidden)
        grad_sent = (
            contract_last(grad_hidden, weight_in)
            .astype(jnp.bfloat16)
            .reshape(experts, capacity, model_width)
        )
        grad_back = lax.all_to_all(grad_sent, "grp", split_axis=0, concat_axis=0, tiled=True)
        grad_doubled = matmul(table, grad_back.reshape(-1, model_width)).reshape(
            2, rows_count, model_width
        )
        grad_probs = picked[0] * grad_gates[0][:, None] + picked[1] * grad_gates[1][:, None]
        grad_logits = (
            probabilities * (grad_probs - jnp.sum(grad_probs * probabilities, -1, keepdims=True))
        ).astype(jnp.bfloat16)
        router_grad = contract_first(normed_two, grad_logits)
        grad_two = grad_doubled[0] + grad_doubled[1] + contract_last(grad_logits, full_router)
        grad_norm_two, gain_moe_grad = norm_backward(grad_two, unit_two, inverse_two, full_gain_moe)
        grad_middle = grad_y + grad_norm_two
        grad_middle_low = grad_middle.astype(jnp.bfloat16)
        proj_grad = contract_first(mixture, grad_middle_low)
        grad_mixture = contract_last(grad_middle_low, full_proj).astype(jnp.bfloat16)
        grad_packed = attend_backward(packed, log_total, grad_mixture)
        qkv_grad = contract_first(normed_one, grad_packed)
        grad_one = contract_last(grad_packed, full_qkv)
        grad_norm_one, gain_attn_grad = norm_backward(
            grad_one, unit_one, inverse_one, full_gain_attn
        )
        grad_states = grad_middle + grad_norm_one
        input_grads.append(grad_states.astype(jnp.bfloat16).reshape(images.shape[1:]))
        dense_full = tuple(
            (
                total + part
                for total, part in zip(
                    dense_full, (qkv_grad, proj_grad, router_grad, gain_attn_grad, gain_moe_grad)
                )
            )
        )
    dense_shard = (
        lax.psum_scatter(
            dense_full[0].astype(jnp.bfloat16), "grp", scatter_dimension=0, tiled=True
        ).astype(jnp.float32),
        lax.psum_scatter(
            dense_full[1].astype(jnp.bfloat16), "grp", scatter_dimension=0, tiled=True
        ).astype(jnp.float32),
        lax.psum_scatter(
            dense_full[2].astype(jnp.bfloat16), "grp", scatter_dimension=0, tiled=True
        ).astype(jnp.float32),
        lax.psum_scatter(
            dense_full[3].astype(jnp.bfloat16), "grp", scatter_dimension=0, tiled=True
        ).astype(jnp.float32),
        lax.psum_scatter(
            dense_full[4].astype(jnp.bfloat16), "grp", scatter_dimension=0, tiled=True
        ).astype(jnp.float32),
    )
    summed = (
        lax.psum(dense_shard[0].astype(jnp.bfloat16), "rep").astype(jnp.float32),
        lax.psum(dense_shard[1].astype(jnp.bfloat16), "rep").astype(jnp.float32),
        lax.psum(dense_shard[2].astype(jnp.bfloat16), "rep").astype(jnp.float32),
        lax.psum(dense_shard[3].astype(jnp.bfloat16), "rep").astype(jnp.float32),
        lax.psum(dense_shard[4].astype(jnp.bfloat16), "rep").astype(jnp.float32),
        lax.psum(in_total[None].astype(jnp.bfloat16), "rep").astype(jnp.float32),
        lax.psum(out_total[None].astype(jnp.bfloat16), "rep").astype(jnp.float32),
    )
    return (
        jnp.stack(outputs),
        jnp.stack(input_grads),
        summed[0],
        summed[1],
        summed[2],
        summed[3],
        summed[4],
        summed[5],
        summed[6],
    )


def solution(mesh):
    placed = (
        P(None, ("rep", "grp"), None, None),
        P("grp", None),
        P("grp", None),
        P("grp", None),
        P("grp"),
        P("grp"),
        P("grp", None, None),
        P("grp", None, None),
        P(None, ("rep", "grp"), None, None),
        P(None, ("rep", "grp"), None, None),
    )
    return jax.shard_map(
        shards,
        mesh=mesh,
        in_specs=placed,
        out_specs=(
            P(None, ("rep", "grp"), None, None),
            P(None, ("rep", "grp"), None, None),
            P("grp", None),
            P("grp", None),
            P("grp", None),
            P("grp"),
            P("grp"),
            P("grp", None, None),
            P("grp", None, None),
        ),
        check_vma=False,
    )
```

profile of v0, /device:TPU:0, one launch (start us, length us, event | category | flops | bytes accessed | tf_op | source)
XLA Modules:
  0.0 941.7 jit_solution(2044510110594368311)
XLA Ops:
  15.1 35.6 %all-reduce.8 = (bf16[768]{0:T(1024)(128)(2,1)S(1)}, bf16[768]{0:T(1024)(128)(2,1)S(1)}) all-reduce(bf16[768]{0:T(1024)(128)(2,1)S(1)} %dynamic-update-slice, bf16[768]{0:T(1024)(128)(2,1)S(1)} %dynamic-update-slice.1), channel_id=1, replica_groups=mesh['rep'=2,'grp'=16] {'grp'}, use_global_device_ids=true, to_apply=%add.3 | all-reduce | flops 1536 | bytes 6144
  52.5 17.4 %all-gather = bf16[16,48,16]{1,2,0:T(8,128)(2,1)S(1)} all-gather(bf16[1,48,16]{1,2,0:T(8,128)(2,1)S(1)} %bitcast.570), channel_id=1, replica_groups=mesh['rep'=2,'grp'=16] {'grp'}, dimensions={0}, use_global_device_ids=true | all-gather | bytes 26112 | tf_op jit(solution)/shard_map/all_gather | solution.py:142
  73.9 3.9 convolution_convert_fusion.2
  81.9 18.2 %all-gather.6.cloned.1.call-done = bf16[768,768]{1,0:T(8,128)(2,1)} async-done(((bf16[48,768]{1,0:T(8,128)(2,1)}), bf16[768,768]{1,0:T(8,128)(2,1)}) %all-gather.6.cloned.1.call-update) | async-done | bytes 1179664 | tf_op jit(solution)/shard_map/all_gather | solution.py:141
  104.0 4.6 all-to-all-start
  108.7 3.9 convolution_convert_fusion
  114.4 12.9 %all-to-all-done = bf16[16,32,768]{2,1,0:T(8,128)(2,1)} async-done(((bf16[16,32,768]{2,1,0:T(8,128)(2,1)}), bf16[16,32,768]{2,1,0:T(8,128)(2,1)}, u32[]{:S(2)}, u32[]{:S(2)}) %all-to-all-start) | async-done | bytes 786464 | tf_op jit(solution)/shard_map/all_to_all | solution.py:164
  127.2 18.4 %multiply_convert_fusion.2 = (bf16[512,3072]{1,0:T(8,128)(2,1)S(1)}, f32[512,3072]{1,0:T(8,128)}, f32[512,3072]{1,0:T(8,128)}) fusion(bf16[512,768]{1,0:T(8,128)(2,1)} %bitcast.16, bf16[1,768,3072]{2,1,0:T(8,128)(2,1)} %param.16), kind=kOutput, calls=%fused_computation.38 | convolution fusion | flops 2518155264 | bytes 21233664 | tf_op jit(solution)/shard_map/dot_general | solution.py:26
  145.7 7.0 fusion.62
  152.7 5.5 all-to-all-start.1
  163.5 13.5 %all-to-all-done.1 = bf16[16,32,768]{2,1,0:T(8,128)(2,1)} async-done(((bf16[16,32,768]{2,1,0:T(8,128)(2,1)}), bf16[16,32,768]{2,1,0:T(8,128)(2,1)}, u32[]{:S(2)}, u32[]{:S(2)}) %all-to-all-start.1) | async-done | bytes 786464 | tf_op jit(solution)/shard_map/all_to_all | solution.py:169
  176.9 3.1 multiply_reduce_fusion.8
  180.3 3.0 convolution_convert_fusion.5
  183.3 6.1 all-to-all-start.6
  190.9 2.6 copy.113
  199.7 8.3 all-to-all-done.6
  208.1 10.2 %add_convert_fusion.5 = bf16[512,3072]{1,0:T(8,128)(2,1)S(1)} fusion(f32[512,3072]{1,0:T(8,128)} %get-tuple-element.55, f32[512,3072]{1,0:T(8,128)} %get-tuple-element.103, bf16[512,768]{1,0:T(8,128)(2,1)} %bitcast.64, bf16[1,3072,768]{2,1,0:T(8,128)(2,1)} %param.17), kind=kOutput, calls=%fused_computation.11 | convolution fusion | flops 2437939200 | bytes 21233664 | tf_op jit(solution)/shard_map/dot_general | solution.py:20
  218.3 7.0 fusion.53
  225.3 5.5 all-to-all-start.7
  233.6 16.1 %all-to-all-done.7 = bf16[16,32,768]{2,1,0:T(8,128)(2,1)} async-done(((bf16[16,32,768]{2,1,0:T(8,128)(2,1)}), bf16[16,32,768]{2,1,0:T(8,128)(2,1)}, u32[]{:S(2)}, u32[]{:S(2)}) %all-to-all-start.7) | async-done | bytes 786464 | tf_op jit(solution)/shard_map/all_to_all | solution.py:216
  251.6 3.5 multiply_reduce_fusion.11
  256.7 5.7 all-to-all-start.2
  268.6 2.7 convolution_convert_fusion.6
  271.3 9.8 %all-to-all-done.2 = bf16[16,32,768]{2,1,0:T(8,128)(2,1)S(1)} async-done(((bf16[16,32,768]{2,1,0:T(8,128)(2,1)}), bf16[16,32,768]{2,1,0:T(8,128)(2,1)S(1)}, u32[]{:S(2)}, u32[]{:S(2)}) %all-to-all-start.2) | async-done | bytes 786464 | tf_op jit(solution)/shard_map/all_to_all | solution.py:164
  281.1 5.5 all-to-all-start.4
  286.6 18.2 %multiply_convert_fusion.1 = (bf16[512,3072]{1,0:T(8,128)(2,1)S(1)}, f32[512,3072]{1,0:T(8,128)}, f32[512,3072]{1,0:T(8,128)}) fusion(bf16[512,768]{1,0:T(8,128)(2,1)S(1)} %bitcast.538, bf16[1,768,3072]{2,1,0:T(8,128)(2,1)} %param.16), kind=kOutput, calls=%fused_computation.25 | convolution fusion | flops 2518155264 | bytes 21233664 | tf_op jit(solution)/shard_map/dot_general | solution.py:26
  306.4 5.9 fusion.65
  313.2 6.2 all-to-all-start.3
  319.4 18.4 %multiply_convert_fusion = (bf16[512,3072]{1,0:T(8,128)(2,1)S(1)}, f32[512,3072]{1,0:T(8,128)}, f32[512,3072]{1,0:T(8,128)}) fusion(bf16[512,768]{1,0:T(8,128)(2,1)} %bitcast.542, bf16[1,768,3072]{2,1,0:T(8,128)(2,1)} %param.16), kind=kOutput, calls=%fused_computation.12 | convolution fusion | flops 2518155264 | bytes 21233664 | tf_op jit(solution)/shard_map/dot_general | solution.py:26
  339.6 5.9 fusion.68
  345.5 6.1 all-to-all-start.5
  354.4 3.0 convolution_convert_fusion.4
  357.4 13.0 %all-to-all-done.5 = bf16[16,32,768]{2,1,0:T(8,128)(2,1)S(1)} async-done(((bf16[16,32,768]{2,1,0:T(8,128)(2,1)}), bf16[16,32,768]{2,1,0:T(8,128)(2,1)S(1)}, u32[]{:S(2)}, u32[]{:S(2)}) %all-to-all-start.5) | async-done | bytes 786464 | tf_op jit(solution)/shard_map/all_to_all | solution.py:169
  370.4 5.5 all-to-all-start.8
  375.9 3.0 multiply_reduce_fusion.6
  379.2 3.0 convolution_convert_fusion.3
  382.1 12.5 %all-to-all-done.8 = bf16[16,32,768]{2,1,0:T(8,128)(2,1)} async-done(((bf16[16,32,768]{2,1,0:T(8,128)(2,1)}), bf16[16,32,768]{2,1,0:T(8,128)(2,1)}, u32[]{:S(2)}, u32[]{:S(2)}) %all-to-all-start.8) | async-done | bytes 786464 | tf_op jit(solution)/shard_map/all_to_all | solution.py:203
  394.7 5.9 all-to-all-start.10
  400.5 10.2 %add_convert_fusion.4 = bf16[512,3072]{1,0:T(8,128)(2,1)S(1)} fusion(f32[512,3072]{1,0:T(8,128)} %get-tuple-element.57, f32[512,3072]{1,0:T(8,128)} %get-tuple-element.116, bf16[512,768]{1,0:T(8,128)(2,1)} %bitcast.82, bf16[1,3072,768]{2,1,0:T(8,128)(2,1)} %param.17), kind=kOutput, calls=%fused_computation.10 | convolution fusion | flops 2437939200 | bytes 21233664 | tf_op jit(solution)/shard_map/dot_general | solution.py:20
  412.4 5.9 fusion.56
  419.2 5.5 all-to-all-start.9
  424.8 8.3 add_convert_fusion.3
  434.7 5.9 fusion.59
  440.6 2.9 all-to-all-done.9
  443.5 5.5 all-to-all-start.11
  452.4 15.4 %all-to-all-done.11 = bf16[16,32,768]{2,1,0:T(8,128)(2,1)} async-done(((bf16[16,32,768]{2,1,0:T(8,128)(2,1)}), bf16[16,32,768]{2,1,0:T(8,128)(2,1)}, u32[]{:S(2)}, u32[]{:S(2)}) %all-to-all-start.11) | async-done | bytes 786464 | tf_op jit(solution)/shard_map/all_to_all | solution.py:216
  469.9 2.8 multiply_add_fusion.1
  472.8 2.8 multiply_add_fusion.2
  508.4 3.0 add_convert_fusion.2
  513.4 6.5 fusion.281
  519.9 6.4 fusion.283
  527.5 5.0 fusion.282
  532.5 6.7 fusion.284
  539.2 7.6 fusion.42
  546.8 12.6 %fusion.43 = bf16[1,3072,768]{2,1,0:T(8,128)(2,1)} fusion(bf16[512,3072]{1,0:T(8,128)(2,1)} %copy-done.49, bf16[512,768]{1,0:T(8,128)(2,1)} %bitcast.545, f32[3072,768]{1,0:T(8,128)} %fusion.283, f32[3072,768]{1,0:T(8,128)} %fusion.284), kind=kOutput, calls=%fused_computation.79 | convolution fusion | flops 2422996992 | bytes 27525120 | tf_op jit(solution)/shard_map/dot_general | solution.py:14
  561.0 70.8 %reduce-scatter.6.cloned.1.call-done = bf16[48,2304]{1,0:T(8,128)(2,1)} async-done(((bf16[768,2304]{1,0:T(8,128)(2,1)}), bf16[48,2304]{1,0:T(8,128)(2,1)}) %reduce-scatter.6.cloned.1.call-update) | async-done | bytes 221200 | tf_op jit(solution)/shard_map/reduce_scatter | solution.py:248
  632.6 55.8 %reduce-scatter.10.cloned.1.call-done = bf16[48,16]{1,0:T(8,128)(2,1)} async-done(((bf16[768,16]{1,0:T(8,128)(2,1)}), bf16[48,16]{1,0:T(8,128)(2,1)}) %reduce-scatter.10.cloned.1.call-update) | async-done | bytes 1552
  689.2 3.5 fusion.278
  692.7 3.5 fusion.279
  698.8 29.5 %all-reduce.7 = (bf16[768]{0:T(1024)(128)(2,1)S(1)}, bf16[768]{0:T(1024)(128)(2,1)S(1)}) all-reduce(bf16[768]{0:T(1024)(128)(2,1)S(1)} %add_convert_fusion.8, bf16[768]{0:T(1024)(128)(2,1)S(1)} %add_convert_fusion.7), channel_id=5, replica_groups=mesh['rep'=2,'grp'=16] {'grp'}, use_global_device_ids=true, to_apply=%region_66.67.clone | all-reduce | flops 1536 | bytes 6144
  728.4 5.3 all-reduce.9
  741.5 177.8 %all-reduce.13.cloned.1.call-done = (bf16[48,2304]{1,0:T(8,128)(2,1)}, bf16[48,768]{1,0:T(8,128)(2,1)}, bf16[1,768,3072]{2,1,0:T(8,128)(2,1)}, bf16[1,3072,768]{2,1,0:T(8,128)(2,1)}) async-done(((bf16[48,2304]{1,0:T(8,128)(2,1)}, bf16[48,768]{1,0:T(8,128)(2,1)}, bf16[1,768,3072]{2,1,0:T(8,128)(2,1)}, bf16[1,3072,768]{2,1,0:T(8,128)(2,1)}), (bf16[48,2304]{1,0:T(8,128)(2,1)}, bf16[48,768]{1,0:T(8,128)(2,1)}, ...) | async-done | bytes 9732112 | tf_op jit(solution)/shard_map/psum | solution.py:265
  922.7 7.4 convert_element_type.550
  930.2 4.5 convert_element_type.553
  (416 shorter events, 116.6 us)
Async XLA Ops:
  7.2 6.2 copy-start.95
  7.2 7.4 copy-start.96
  7.2 7.6 copy-start.97
  7.2 43.5 %copy-start.10 = (bf16[3,1,197,768]{3,2,1,0:T(8,128)(2,1)S(1)}, bf16[3,1,197,768]{3,2,1,0:T(8,128)(2,1)}, u32[]{:S(2)}) copy-start(bf16[3,1,197,768]{3,2,1,0:T(8,128)(2,1)} %param.10) | copy-start | bytes 2723332
  7.2 45.2 %copy-start.94 = (bf16[48,16]{0,1:T(8,128)(2,1)S(1)}, bf16[48,16]{0,1:T(8,128)(2,1)}, u32[]{:S(2)}) copy-start(bf16[48,16]{0,1:T(8,128)(2,1)} %param.13) | copy-start | bytes 4612
  7.2 66.7 %all-gather.4.cloned.1.call-start = ((), (), s32[]{:S(2)}) async-start(), calls=%async_computation.15 | async-start | bytes 3760128 | tf_op jit(solution)/shard_map/all_gather | solution.py:140
  8.0 92.1 %all-gather.6.cloned.1.call-start = ((), (), s32[]{:S(2)}) async-start(), calls=%async_computation.16 | async-start | bytes 1253376 | tf_op jit(solution)/shard_map/all_gather | solution.py:141
  50.7 110.8 %copy-start.71 = (f32[768]{0:T(1024)}, f32[768]{0:T(1024)S(1)}, u32[]{:S(2)}) copy-start(f32[768]{0:T(1024)S(1)} %convert_element_type.439) | copy-start | bytes 9220
  73.3 35.4 %copy-start.89 = (f32[197]{0:T(256)}, f32[197]{0:T(256)S(1)}, u32[]{:S(2)}) copy-start(f32[197]{0:T(256)S(1)} %get-tuple-element.134) | copy-start | bytes 2368
  73.3 88.2 %copy-start.81 = (f32[197]{0:T(256)}, f32[197]{0:T(256)S(1)}, u32[]{:S(2)}) copy-start(f32[197]{0:T(256)S(1)} %get-tuple-element.135) | copy-start | bytes 2368
  73.3 6.5 copy-start.83
  73.8 6.1 copy-start.87
  79.3 22.6 %copy-start.20 = (bf16[197,2304]{0,1:T(8,128)(2,1)}, bf16[197,2304]{0,1:T(8,128)(2,1)S(1)}, u32[]{:S(2)}) copy-start(bf16[197,2304]{0,1:T(8,128)(2,1)S(1)} %copy.108) | copy-start | bytes 2723332
  81.3 20.8 %copy-start.73 = (f32[12,197]{1,0:T(8,128)}, f32[12,197]{1,0:T(8,128)S(1)}, u32[]{:S(2)}) copy-start(f32[12,197]{1,0:T(8,128)S(1)} %log_add_fusion.2) | copy-start | bytes 28372
  81.9 30.7 %copy-start.40 = (bf16[12,64,197]{2,1,0:T(8,128)(2,1)}, bf16[12,64,197]{2,1,0:T(8,128)(2,1)S(1)}, u32[]{:S(2)}) copy-start(bf16[12,64,197]{2,1,0:T(8,128)(2,1)S(1)} %convolution_convert_fusion.11) | copy-start | bytes 907780
  102.3 11.8 %copy-start.57 = (bf16[197,768]{1,0:T(8,128)(2,1)}, bf16[197,768]{1,0:T(8,128)(2,1)S(1)}, u32[]{:S(2)}) copy-start(bf16[197,768]{1,0:T(8,128)(2,1)S(1)} %multiply_convert_fusion.14) | copy-start | bytes 907780
  104.0 23.3 %all-to-all-start = ((bf16[16,32,768]{2,1,0:T(8,128)(2,1)}), bf16[16,32,768]{2,1,0:T(8,128)(2,1)}, u32[]{:S(2)}, u32[]{:S(2)}) async-start(bf16[16,32,768]{2,1,0:T(8,128)(2,1)} %bitcast.15), calls=%async_computation | async-start | bytes 1572864 | tf_op jit(solution)/shard_map/all_to_all | solution.py:164
  108.6 52.9 %copy-start.85 = (f32[197]{0:T(256)}, f32[197]{0:T(256)S(1)}, u32[]{:S(2)}) copy-start(f32[197]{0:T(256)S(1)} %add_rsqrt_fusion.3) | copy-start | bytes 2368
  114.1 45.1 %copy-start.22 = (bf16[197,2304]{0,1:T(8,128)(2,1)}, bf16[197,2304]{0,1:T(8,128)(2,1)S(1)}, u32[]{:S(2)}) copy-start(bf16[197,2304]{0,1:T(8,128)(2,1)S(1)} %copy.117) | copy-start | bytes 2723332
  145.7 7.0 copy-start.98
  152.7 24.3 %all-to-all-start.1 = ((bf16[16,32,768]{2,1,0:T(8,128)(2,1)}), bf16[16,32,768]{2,1,0:T(8,128)(2,1)}, u32[]{:S(2)}, u32[]{:S(2)}) async-start(bf16[16,32,768]{2,1,0:T(8,128)(2,1)} %bitcast.19), calls=%async_computation.1 | async-start | bytes 1572864 | tf_op jit(solution)/shard_map/all_to_all | solution.py:169
  163.5 25.9 %copy-start.6 = (bf16[768,768]{1,0:T(8,128)(2,1)S(1)}, bf16[768,768]{1,0:T(8,128)(2,1)}, u32[]{:S(2)}) copy-start(bf16[768,768]{1,0:T(8,128)(2,1)} %all-gather.6.cloned.1.call-done) | copy-start | bytes 3538948
  183.3 24.8 %all-to-all-start.6 = ((bf16[16,32,768]{2,1,0:T(8,128)(2,1)}), bf16[16,32,768]{2,1,0:T(8,128)(2,1)}, u32[]{:S(2)}, u32[]{:S(2)}) async-start(bf16[16,32,768]{2,1,0:T(8,128)(2,1)} %bitcast.550), calls=%async_computation.6 | async-start | bytes 1572864 | tf_op jit(solution)/shard_map/all_to_all | solution.py:203
  190.9 279.1 %copy-start.13 = (f32[197,768]{1,0:T(8,128)}, f32[197,768]{1,0:T(8,128)S(1)}, u32[]{:S(2)}) copy-start(f32[197,768]{1,0:T(8,128)S(1)} %get-tuple-element.111) | copy-start | bytes 1815556
  218.3 7.0 copy-start.46
  225.3 24.3 %all-to-all-start.7 = ((bf16[16,32,768]{2,1,0:T(8,128)(2,1)}), bf16[16,32,768]{2,1,0:T(8,128)(2,1)}, u32[]{:S(2)}, u32[]{:S(2)}) async-start(bf16[16,32,768]{2,1,0:T(8,128)(2,1)} %bitcast.549), calls=%async_computation.7 | async-start | bytes 1572864 | tf_op jit(solution)/shard_map/all_to_all | solution.py:216
  232.4 19.2 %copy-start.36 = (f32[394,768]{1,0:T(8,128)S(1)}, f32[394,768]{1,0:T(8,128)}, u32[]{:S(2)}) copy-start(f32[394,768]{1,0:T(8,128)} %get-tuple-element.105) | copy-start | bytes 3631108
  233.6 23.2 %copy-start.79 = (bf16[197,16]{0,1:T(8,128)(2,1)}, bf16[197,16]{0,1:T(8,128)(2,1)S(1)}, u32[]{:S(2)}) copy-start(bf16[197,16]{0,1:T(8,128)(2,1)S(1)} %multiply_convert_fusion.17) | copy-start | bytes 18916
  256.7 24.3 %all-to-all-start.2 = ((bf16[16,32,768]{2,1,0:T(8,128)(2,1)}), bf16[16,32,768]{2,1,0:T(8,128)(2,1)S(1)}, u32[]{:S(2)}, u32[]{:S(2)}) async-start(bf16[16,32,768]{2,1,0:T(8,128)(2,1)} %bitcast.36), calls=%async_computation.2 | async-start | bytes 1572864 | tf_op jit(solution)/shard_map/all_to_all | solution.py:164
  281.1 23.7 %copy-start.44 = (bf16[16,32,768]{2,1,0:T(8,128)(2,1)}, bf16[16,32,768]{2,1,0:T(8,128)(2,1)S(1)}, u32[]{:S(2)}) copy-start(bf16[16,32,768]{2,1,0:T(8,128)(2,1)S(1)} %all-to-all-done.2) | copy-start | bytes 2359300
  281.1 31.2 %all-to-all-start.4 = ((bf16[16,32,768]{2,1,0:T(8,128)(2,1)}), bf16[16,32,768]{2,1,0:T(8,128)(2,1)S(1)}, u32[]{:S(2)}, u32[]{:S(2)}) async-start(bf16[16,32,768]{2,1,0:T(8,128)(2,1)} %bitcast.552), calls=%async_computation.4 | async-start | bytes 1572864 | tf_op jit(solution)/shard_map/all_to_all | solution.py:164
  313.2 32.4 %all-to-all-start.3 = ((bf16[16,32,768]{2,1,0:T(8,128)(2,1)}), bf16[16,32,768]{2,1,0:T(8,128)(2,1)S(1)}, u32[]{:S(2)}, u32[]{:S(2)}) async-start(bf16[16,32,768]{2,1,0:T(8,128)(2,1)} %bitcast.38), calls=%async_computation.3 | async-start | bytes 1572864 | tf_op jit(solution)/shard_map/all_to_all | solution.py:169
  339.6 12.1 %copy-start.53 = (bf16[197,768]{1,0:T(8,128)(2,1)S(1)}, bf16[197,768]{1,0:T(8,128)(2,1)}, u32[]{:S(2)}) copy-start(bf16[197,768]{1,0:T(8,128)(2,1)} %get-tuple-element.74) | copy-start | bytes 907780
  345.5 6.4 copy-start.45
  345.5 24.8 %all-to-all-start.5 = ((bf16[16,32,768]{2,1,0:T(8,128)(2,1)}), bf16[16,32,768]{2,1,0:T(8,128)(2,1)S(1)}, u32[]{:S(2)}, u32[]{:S(2)}) async-start(bf16[16,32,768]{2,1,0:T(8,128)(2,1)} %bitcast.548), calls=%async_computation.5 | async-start | bytes 1572864 | tf_op jit(solution)/shard_map/all_to_all | solution.py:169
  370.4 24.3 %all-to-all-start.8 = ((bf16[16,32,768]{2,1,0:T(8,128)(2,1)}), bf16[16,32,768]{2,1,0:T(8,128)(2,1)}, u32[]{:S(2)}, u32[]{:S(2)}) async-start(bf16[16,32,768]{2,1,0:T(8,128)(2,1)} %bitcast.547), calls=%async_computation.8 | async-start | bytes 1572864 | tf_op jit(solution)/shard_map/all_to_all | solution.py:203
  394.7 24.6 %all-to-all-start.10 = ((bf16[16,32,768]{2,1,0:T(8,128)(2,1)}), bf16[16,32,768]{2,1,0:T(8,128)(2,1)S(1)}, u32[]{:S(2)}, u32[]{:S(2)}) async-start(bf16[16,32,768]{2,1,0:T(8,128)(2,1)} %bitcast.551), calls=%async_computation.10 | async-start | bytes 1572864 | tf_op jit(solution)/shard_map/all_to_all | solution.py:203
  419.2 24.3 %all-to-all-start.9 = ((bf16[16,32,768]{2,1,0:T(8,128)(2,1)}), bf16[16,32,768]{2,1,0:T(8,128)(2,1)}, u32[]{:S(2)}, u32[]{:S(2)}) async-start(bf16[16,32,768]{2,1,0:T(8,128)(2,1)} %bitcast.553), calls=%async_computation.9 | async-start | bytes 1572864 | tf_op jit(solution)/shard_map/all_to_all | solution.py:216
  434.7 16.4 %copy-start.29 = (f32[197,768]{1,0:T(8,128)S(1)}, f32[197,768]{1,0:T(8,128)}, u32[]{:S(2)}) copy-start(f32[197,768]{1,0:T(8,128)} %copy-done.28) | copy-start | bytes 1815556
  443.5 24.3 %all-to-all-start.11 = ((bf16[16,32,768]{2,1,0:T(8,128)(2,1)}), bf16[16,32,768]{2,1,0:T(8,128)(2,1)}, u32[]{:S(2)}, u32[]{:S(2)}) async-start(bf16[16,32,768]{2,1,0:T(8,128)(2,1)} %bitcast.546), calls=%async_computation.11 | async-start | bytes 1572864 | tf_op jit(solution)/shard_map/all_to_all | solution.py:216
  449.1 111.9 %reduce-scatter.8.cloned.1.call-start = ((), (), s32[]{:S(2)}) async-start(), calls=%async_computation.18 | async-start | bytes 1253376 | tf_op jit(solution)/shard_map/reduce_scatter | solution.py:251
  469.9 6.5 copy-start.7
  502.0 129.8 %reduce-scatter.6.cloned.1.call-start = ((), (), s32[]{:S(2)}) async-start(), calls=%async_computation.17 | async-start | bytes 3760128 | tf_op jit(solution)/shard_map/reduce_scatter | solution.py:248
  511.5 176.9 %reduce-scatter.10.cloned.1.call-start = ((), (), s32[]{:S(2)}) async-start(), calls=%async_computation.19 | async-start | bytes 208896
  513.4 6.5 copy-start.99
  519.9 6.4 copy-start.56
  519.9 6.6 copy-start.54
  527.5 391.8 %all-reduce.13.cloned.1.call-start = ((), (), s32[]{:S(2)}) async-start(), calls=%async_computation.20 | async-start | bytes 19464192 | tf_op jit(solution)/shard_map/psum | solution.py:265
  527.5 11.7 %slice-start = ((s8[9437184]{0:T(1024)(128)(4,1)}), s8[4194304]{0:T(1024)(128)(4,1)S(1)}, s32[]{:S(2)}) async-start(s8[9437184]{0:T(1024)(128)(4,1)} %bitcast.501), calls=%async_computation.21 | async-start | bytes 8388608
  527.5 11.7 %slice-start.1 = ((s8[9437184]{0:T(1024)(128)(4,1)}), s8[4194304]{0:T(1024)(128)(4,1)S(1)}, s32[]{:S(2)}) async-start(s8[9437184]{0:T(1024)(128)(4,1)} %bitcast.501), calls=%async_computation.22 | async-start | bytes 8388608
  532.5 6.7 slice-start.2
  631.8 57.4 %copy-start.17 = (bf16[1,197,3,12,64]{1,4,3,2,0:T(8,128)(2,1)S(1)}, bf16[1,197,3,12,64]{1,4,3,2,0:T(8,128)(2,1)}, u32[]{:S(2)}) copy-start(bf16[1,197,3,12,64]{1,4,3,2,0:T(8,128)(2,1)} %copy-done.16) | copy-start | bytes 2723332
  631.8 60.8 %copy-start.19 = (bf16[1,197,3,12,64]{1,4,3,2,0:T(8,128)(2,1)S(1)}, bf16[1,197,3,12,64]{1,4,3,2,0:T(8,128)(2,1)}, u32[]{:S(2)}) copy-start(bf16[1,197,3,12,64]{1,4,3,2,0:T(8,128)(2,1)} %copy-done.18) | copy-start | bytes 2723332
  689.2 7.1 copy-start.12
  689.2 7.1 copy-start.15
  689.2 7.1 copy-start.38
  692.7 6.1 copy-start.62
  696.3 39.1 %copy-start.69 = (bf16[1,1,197,768]{3,2,1,0:T(8,128)(2,1)S(1)}, bf16[1,1,197,768]{3,2,1,0:T(8,128)(2,1)}, u32[]{:S(2)}) copy-start(bf16[1,1,197,768]{3,2,1,0:T(8,128)(2,1)} %get-tuple-element.68) | copy-start | bytes 907780
  696.3 39.1 %copy-start.70 = (bf16[1,1,197,768]{3,2,1,0:T(8,128)(2,1)S(1)}, bf16[1,1,197,768]{3,2,1,0:T(8,128)(2,1)}, u32[]{:S(2)}) copy-start(bf16[1,1,197,768]{3,2,1,0:T(8,128)(2,1)} %get-tuple-element.70) | copy-start | bytes 907780
  696.3 41.1 %copy-start.27 = (f32[197,768]{1,0:T(8,128)S(1)}, f32[197,768]{1,0:T(8,128)}, u32[]{:S(2)}) copy-start(f32[197,768]{1,0:T(8,128)} %get-tuple-element.69) | copy-start | bytes 1815556
  696.3 42.4 %copy-start.32 = (f32[197,768]{1,0:T(8,128)S(1)}, f32[197,768]{1,0:T(8,128)}, u32[]{:S(2)}) copy-start(f32[197,768]{1,0:T(8,128)} %copy-done.30) | copy-start | bytes 1815556
  696.3 42.4 %copy-start.34 = (f32[197,768]{1,0:T(8,128)S(1)}, f32[197,768]{1,0:T(8,128)}, u32[]{:S(2)}) copy-start(f32[197,768]{1,0:T(8,128)} %get-tuple-element.63) | copy-start | bytes 1815556
  921.0 9.1 slice-start.3
  922.7 7.4 slice-start.4
  (61 other events, 172.9 us)
Sparse Core Ops, SparseCore 0:
  10.3 49.9 all-gather.3
  62.7 37.3 all-gather.5
  502.1 58.8 reduce-scatter.7
  564.7 67.0 reduce-scatter.5
  635.7 52.6 reduce-scatter.9
  691.5 227.7 all-reduce.12
where the time goes:
time: 950 us; the launch traced here: 942 us
  waiting for transfers between devices  431 us (45%)
  matrix products  257 us (27%)
  blocking collectives  87.8 us (9%)
  starting transfers between devices  68 us (7%)
  other arithmetic  47.9 us (5%)
  local copies, waits for them, and re-layouts  32.9 us (3%)
  between operations  17.6 us (2%)
    psum x1, waiting for transfers between devices, shards(): lax.psum(dense_shard[0].astype(jnp.bfloat16), 'rep').astype(jnp.float32)  178 us
    dot_general x21, matrix products, matmul(): return jnp.dot(left, right, preferred_element_type=jnp.float32)  103 us
    reduce_scatter x1, waiting for transfers between devices, shards(): lax.psum_scatter(dense_full[0].astype(jnp.bfloat16), 'grp', scatter_dimen...  70.8 us
    dot_general x21, matrix products, contract_first(): lax.dot_general(left, right, (((0,), (0,)), ((), ())), preferred_element_...  68.4 us
    unnamed x2, blocking collectives  65.1 us
    dot_general x15, matrix products, contract_last(): lax.dot_general(left, right, (((1,), (1,)), ((), ())), preferred_element_...  61.1 us
    unnamed x7, waiting for transfers between devices  57.2 us
    all_to_all x3, waiting for transfers between devices, shards(): lax.all_to_all(grad_sent, 'grp', split_axis=0, concat_axis=0, tiled=True)  34.4 us
  transfers between devices with their start and end apart: 18, of which 15 were waited for; matrix products, arithmetic and copies ran while one was open for 23% of the time, Pallas kernels for 0%

commit v1 on v0

v1 whole, which is shorter than its diff:
```python
import jax
import jax.numpy as jnp
from jax import lax
from jax.sharding import PartitionSpec as P

HEADS = 12
EPSILON = 1e-06
BF = jnp.bfloat16
F32 = jnp.float32


def dot_tn(left, right):
    return lax.dot_general(left, right, (((0,), (0,)), ((), ())), preferred_element_type=F32)


def dot_nt(left, right):
    return lax.dot_general(left, right, (((1,), (1,)), ((), ())), preferred_element_type=F32)


def dot_nn(left, right):
    return jnp.dot(left, right, preferred_element_type=F32)


def normalize(values):
    center = values - jnp.mean(values, -1, keepdims=True)
    inverse = lax.rsqrt(jnp.mean(center * center, -1, keepdims=True) + EPSILON)
    return center * inverse, inverse


def norm_backward(grad_rows, unit_rows, inverse, gain_row):
    scaled = grad_rows * gain_row
    inner = (
        scaled
        - jnp.mean(scaled, -1, keepdims=True)
        - unit_rows * jnp.mean(scaled * unit_rows, -1, keepdims=True)
    )
    return inner * inverse, jnp.sum(grad_rows * unit_rows, 0)


def split_heads(packed):
    seq = packed.shape[0]
    head_dim = packed.shape[1] // (3 * HEADS)
    pieces = packed.reshape(seq, 3, HEADS, head_dim)
    return pieces[:, 0], pieces[:, 1], pieces[:, 2], head_dim ** (-0.5)


def attend_forward(packed):
    query, keys, values, factor = split_heads(packed)
    scores = jnp.einsum("shd,thd->hst", query, keys, preferred_element_type=F32) * factor
    highest = jnp.max(scores, -1, keepdims=True)
    log_total = highest + jnp.log(jnp.sum(jnp.exp(scores - highest), -1, keepdims=True))
    weights = jnp.exp(scores - log_total).astype(BF)
    mixture = jnp.einsum("hst,thd->shd", weights, values, preferred_element_type=F32)
    return mixture.reshape(packed.shape[0], -1).astype(BF), log_total


def attend_backward(packed, log_total, grad_mixture):
    query, keys, values, factor = split_heads(packed)
    scores = jnp.einsum("shd,thd->hst", query, keys, preferred_element_type=F32) * factor
    weights = jnp.exp(scores - log_total)
    low = weights.astype(BF)
    grad_heads = grad_mixture.reshape(query.shape)
    grad_values = jnp.einsum("hst,shd->thd", low, grad_heads, preferred_element_type=F32)
    grad_weights = jnp.einsum("shd,thd->hst", grad_heads, values, preferred_element_type=F32)
    grad_scores = (
        weights * (grad_weights - jnp.sum(grad_weights * weights, -1, keepdims=True))
    ).astype(BF)
    grad_query = jnp.einsum("hst,thd->shd", grad_scores, keys, preferred_element_type=F32) * factor
    grad_keys = jnp.einsum("hst,shd->thd", grad_scores, query, preferred_element_type=F32) * factor
    stacked = jnp.stack([grad_query, grad_keys, grad_values], 1)
    return stacked.reshape(packed.shape[0], -1).astype(BF)


def slot_tables(routes, experts, capacity):
    micro, rows = routes.shape[:2]
    ordering = jnp.concatenate([routes[:, :, 0], routes[:, :, 1]], 1)
    onehot = (ordering[:, :, None] == jnp.arange(experts, dtype=jnp.int32)).astype(BF)
    count = 2 * rows
    earlier = (jnp.arange(count)[:, None] > jnp.arange(count)[None, :]).astype(BF)
    before = jnp.einsum("ab,mbe->mae", earlier, onehot, preferred_element_type=F32)
    rank = jnp.sum(before * onehot, -1).astype(jnp.int32)
    target = jnp.where(rank < capacity, ordering * capacity + rank, -1)
    slots = jnp.arange(experts * capacity, dtype=jnp.int32)[None, :, None]
    first, second = target[:, None, :rows], target[:, None, rows:]
    return ((slots == first) | (slots == second)).astype(BF)


def exchange(blocks):
    return lax.all_to_all(blocks, "grp", split_axis=0, concat_axis=0, tiled=True)


def expert_rows(slots_in, grad_in, weight_in, weight_out, full_router, mine):
    hidden = dot_nn(slots_in, weight_in)
    cumulative = 0.5 * (1.0 + lax.erf(hidden * (0.5**0.5)))
    active = (hidden * cumulative).astype(BF)
    slope = cumulative + hidden * jnp.exp(-0.5 * hidden * hidden) * 0.3989422804014327
    probs = jax.nn.softmax(dot_nn(slots_in, full_router), axis=-1)
    here = (jnp.arange(probs.shape[1], dtype=jnp.int32) == mine).astype(F32)[None]
    gate = jnp.sum(probs * here, -1, keepdims=True)
    grad_result = (gate * grad_in.astype(F32)).astype(BF)
    grad_hidden = (dot_nt(grad_result, weight_out) * slope).astype(BF)
    return active, grad_hidden, grad_result, gate, probs, here


def shards(images, attn_qkv, attn_proj, router, gain_attn, gain_moe, expert_in, expert_out, routes, cotangent):
    experts = lax.axis_size("grp")
    replicas = lax.axis_size("rep")
    mine = lax.axis_index("grp")
    micro_count, _, seq, width = images.shape
    capacity = max(2, 8 * seq * images.shape[1] // (3 * experts))
    weight_in, weight_out = expert_in[0], expert_out[0]
    split = attn_qkv.shape[1]

    tables = slot_tables(routes.reshape(micro_count, seq, 2), experts, capacity)
    grad_y = cotangent.reshape(micro_count, seq, width)

    def pack(m, rows):
        return dot_nn(tables[m], rows).astype(BF).reshape(experts, capacity, width)

    def unpack(m, blocks):
        return dot_tn(tables[m], blocks.reshape(experts * capacity, width))

    dense = jnp.concatenate([attn_qkv, attn_proj], 1)
    small = jnp.concatenate([router, gain_attn[:, None], gain_moe[:, None]], 1)
    small = jnp.pad(small, ((0, 0), (0, 128 - small.shape[1])))
    full = lax.all_gather(jnp.concatenate([dense, small], 1), "grp", axis=0, tiled=True)
    full_qkv = full[:, :split]
    full_proj = full[:, split : split + width]
    full_small = full[:, split + width :]
    full_router = full_small[:, :experts]
    gain_one = full_small[:, experts].astype(F32)[None]
    gain_two = full_small[:, experts + 1].astype(F32)[None]

    grads_in = [exchange(pack(m, grad_y[m])).reshape(-1, width) for m in range(micro_count)]

    saved, slots_in = [], []
    for m in range(micro_count):
        states = images[m].reshape(seq, width).astype(F32)
        unit_one, inverse_one = normalize(states)
        normed_one = (unit_one * gain_one).astype(BF)
        packed = dot_nn(normed_one, full_qkv).astype(BF)
        mixture, log_total = attend_forward(packed)
        middle = states + dot_nn(mixture, full_proj)
        unit_two, inverse_two = normalize(middle)
        normed_two = (unit_two * gain_two).astype(BF)
        slots_in.append(exchange(pack(m, normed_two)).reshape(-1, width))
        saved.append((unit_one, inverse_one, normed_one, packed, mixture, log_total, middle, unit_two, inverse_two))

    in_terms, out_terms = [], []
    router_total = 0.0
    outputs, input_grads = [], []
    backs, results = [], []
    for m in range(micro_count):
        x, g = slots_in[m], grads_in[m]
        active, grad_hidden, grad_result, gate, probs, here = expert_rows(
            x, g, weight_in, weight_out, full_router, mine
        )
        result = dot_nn(active, weight_out)
        grad_gate = jnp.sum(g.astype(F32) * result, -1, keepdims=True)
        grad_logit = (grad_gate * gate * (here - probs)).astype(BF)
        back = dot_nt(grad_hidden, weight_in) + dot_nt(grad_logit, full_router)
        backs.append(exchange(back.astype(BF).reshape(experts, capacity, width)))
        results.append(exchange((gate * result).astype(BF).reshape(experts, capacity, width)))
        router_total = router_total + dot_tn(x, grad_logit)
        in_terms.append((x, grad_hidden))
        out_terms.append((active, grad_result))
        if replicas == 2:
            x, g = lax.ppermute(x, "rep", [(0, 1), (1, 0)]), lax.ppermute(g, "rep", [(0, 1), (1, 0)])
            active, grad_hidden, grad_result, *_ = expert_rows(x, g, weight_in, weight_out, full_router, mine)
            in_terms.append((x, grad_hidden))
            out_terms.append((active, grad_result))

    def total(terms):
        left, right = zip(*terms)
        return dot_tn(jnp.concatenate(left, 0), jnp.concatenate(right, 0))[None]

    grad_in, grad_out = total(in_terms), total(out_terms)
    if replicas != 2:
        grad_in = lax.psum(grad_in.astype(BF), "rep").astype(F32)
        grad_out = lax.psum(grad_out.astype(BF), "rep").astype(F32)

    one_rows, packed_rows, mix_rows, mid_rows = [], [], [], []
    gain_one_total, gain_two_total = 0.0, 0.0
    for m in range(micro_count):
        unit_one, inverse_one, normed_one, packed, mixture, log_total, middle, unit_two, inverse_two = saved[m]
        grad_two = unpack(m, backs[m])
        grad_norm, gain_part = norm_backward(grad_two, unit_two, inverse_two, gain_two)
        gain_two_total = gain_two_total + gain_part
        grad_middle = grad_y[m].astype(F32) + grad_norm
        low = grad_middle.astype(BF)
        grad_mixture = dot_nt(low, full_proj).astype(BF)
        grad_packed = attend_backward(packed, log_total, grad_mixture)
        grad_one = dot_nt(grad_packed, full_qkv)
        grad_norm, gain_part = norm_backward(grad_one, unit_one, inverse_one, gain_one)
        gain_one_total = gain_one_total + gain_part
        input_grads.append((grad_middle + grad_norm).astype(BF).reshape(images.shape[1:]))
        one_rows.append(normed_one)
        packed_rows.append(grad_packed)
        mix_rows.append(mixture)
        mid_rows.append(low)
        outputs.append((middle + unpack(m, results[m])).astype(BF).reshape(images.shape[1:]))

    grad_qkv = dot_tn(jnp.concatenate(one_rows, 0), jnp.concatenate(packed_rows, 0))
    grad_proj = dot_tn(jnp.concatenate(mix_rows, 0), jnp.concatenate(mid_rows, 0))
    tail = jnp.concatenate([router_total, gain_one_total[:, None], gain_two_total[:, None]], 1)
    tail = jnp.pad(tail, ((0, 0), (0, 128 - tail.shape[1])))
    sums = jnp.concatenate([grad_qkv, grad_proj, tail], 1).astype(BF)
    sums = lax.psum_scatter(sums, "grp", scatter_dimension=0, tiled=True)
    sums = lax.psum(sums, "rep").astype(F32)
    return (
        jnp.stack(outputs),
        jnp.stack(input_grads),
        sums[:, :split],
        sums[:, split : split + width],
        sums[:, split + width : split + width + experts],
        sums[:, split + width + experts],
        sums[:, split + width + experts + 1],
        grad_in,
        grad_out,
    )


def solution(mesh):
    tokens = P(None, ("rep", "grp"), None, None)
    rows = P("grp", None)
    expert = P("grp", None, None)
    return jax.shard_map(
        shards,
        mesh=mesh,
        in_specs=(tokens, rows, rows, rows, P("grp"), P("grp"), expert, expert, tokens, tokens),
        out_specs=(tokens, tokens, rows, rows, rows, P("grp"), P("grp"), expert, expert),
        check_vma=False,
    )
```

time: 950 us -> 661 us (0.70)
  waiting for transfers between devices: 431 us -> 206 us
  blocking collectives: 87.8 us -> 0 us
    psum x1, waiting for transfers between devices: 178 us -> 21.2 us  [shards(): sums = lax.psum(sums, 'rep').astype(F32)]
    unnamed x2 -> x0, blocking collectives: 65.1 us -> none
    unnamed x7 -> x3, waiting for transfers between devices: 57.2 us -> 0.05 us
    reduce_scatter x2 -> x1, waiting for transfers between devices: 72.3 us -> 16.5 us  [shards(): sums = lax.psum_scatter(sums, 'grp', scatter_dimension=0, tiled=True)]
    ppermute x0 -> x6, waiting for transfers between devices: none -> 43.3 us  [the longest x3 43.3 us: shards(): lax.ppermute(x, 'rep', [(0, 1), (1, 0)])]
    all_gather x2 -> x1, waiting for transfers between devices: 18.2 us -> 56 us  [shards(): lax.all_gather(jnp.concatenate([dense, small], 1), 'grp', axis=0, tiled=T...]
    all_to_all x12, waiting for transfers between devices: 105 us -> 69.3 us  [exchange(): lax.all_to_all(blocks, 'grp', split_axis=0, concat_axis=0, tiled=True)]
    all_gather x1 -> x0, blocking collectives: 17.4 us -> none  [shards(): lax.all_gather(router, 'grp', axis=0, tiled=True)]
  transfers between devices with their start and end apart: 18 -> 21, of which waited for: 15 -> 15; matrix products, arithmetic and copies ran while one was open for 23% -> 51% of each run, Pallas kernels for 0% -> 0%
where the time goes in v1:
time: 661 us; the launch traced here: 650 us
  matrix products  262 us (40%)
  waiting for transfers between devices  206 us (31%)
  starting transfers between devices  77.3 us (12%)
  other arithmetic  47.3 us (7%)
  local copies, waits for them, and re-layouts  41.2 us (6%)
  between operations  15.7 us (2%)
    dot_general x27, matrix products, dot_nn(): return jnp.dot(left, right, preferred_element_type=F32)  92.7 us
    dot_general x18, matrix products, dot_nt(): lax.dot_general(left, right, (((1,), (1,)), ((), ())), preferred_element_...  75.5 us
    all_to_all x12, starting transfers between devices, exchange(): lax.all_to_all(blocks, 'grp', split_axis=0, concat_axis=0, tiled=True)  69.9 us
    dot_general x13, matrix products, dot_tn(): lax.dot_general(left, right, (((0,), (0,)), ((), ())), preferred_element_...  69.8 us
    all_to_all x12, waiting for transfers between devices, exchange(): lax.all_to_all(blocks, 'grp', split_axis=0, concat_axis=0, tiled=True)  69.3 us
    all_gather x1, waiting for transfers between devices, shards(): lax.all_gather(jnp.concatenate([dense, small], 1), 'grp', axis=0, tiled=T...  56 us
    ppermute x3, waiting for transfers between devices, shards(): lax.ppermute(x, 'rep', [(0, 1), (1, 0)])  43.3 us
    psum x1, waiting for transfers between devices, shards(): sums = lax.psum(sums, 'rep').astype(F32)  21.2 us
  transfers between devices with their start and end apart: 21, of which 15 were waited for; matrix products, arithmetic and copies ran while one was open for 51% of the time, Pallas kernels for 0%

profile of v1, /device:TPU:0, one launch (start us, length us, event | category | flops | bytes accessed | tf_op | source)
XLA Modules:
  0.0 650.1 jit_solution(11290442664201625727)
XLA Ops:
  13.7 7.4 %all-to-all-start.6 = ((bf16[16,32,768]{2,1,0:T(8,128)(2,1)}), bf16[16,32,768]{2,1,0:T(8,128)(2,1)}, u32[]{:S(2)}, u32[]{:S(2)}) async-start(bf16[16,32,768]{2,1,0:T(8,128)(2,1)} %bitcast.48), calls=%async_computation.6 | async-start | bytes 1572864 | tf_op jit(solution)/shard_map/all_to_all | solution.py:89
  24.1 56.0 %all-gather.2.cloned.1.call-done = bf16[768,3200]{1,0:T(8,128)(2,1)} async-done(((bf16[48,3200]{1,0:T(8,128)(2,1)}), bf16[768,3200]{1,0:T(8,128)(2,1)}) %all-gather.2.cloned.1.call-update) | async-done | bytes 4915216 | tf_op jit(solution)/shard_map/all_gather | solution.py:126
  82.5 3.1 convolution_convert_fusion.3
  88.8 4.7 convolution_convert_fusion.2
  93.5 2.4 copy.84
  100.9 4.3 all-to-all-start.8
  107.2 2.3 convolution_convert_fusion.15
  109.5 2.9 convolution_convert_fusion.1
  112.5 11.4 %all-to-all-done.8 = bf16[16,32,768]{2,1,0:T(8,128)(2,1)} async-done(((bf16[16,32,768]{2,1,0:T(8,128)(2,1)}), bf16[16,32,768]{2,1,0:T(8,128)(2,1)}, u32[]{:S(2)}, u32[]{:S(2)}) %all-to-all-start.8) | async-done | bytes 786464 | tf_op jit(solution)/shard_map/all_to_all | solution.py:89
  123.9 5.7 all-to-all-start
  136.7 11.7 %all-to-all-done = bf16[16,32,768]{2,1,0:T(8,128)(2,1)} async-done(((bf16[16,32,768]{2,1,0:T(8,128)(2,1)}), bf16[16,32,768]{2,1,0:T(8,128)(2,1)}, u32[]{:S(2)}, u32[]{:S(2)}) %all-to-all-start) | async-done | bytes 786464 | tf_op jit(solution)/shard_map/all_to_all | solution.py:89
  148.4 5.5 all-to-all-start.2
  160.3 12.3 %all-to-all-done.2 = bf16[16,32,768]{2,1,0:T(8,128)(2,1)} async-done(((bf16[16,32,768]{2,1,0:T(8,128)(2,1)}), bf16[16,32,768]{2,1,0:T(8,128)(2,1)}, u32[]{:S(2)}, u32[]{:S(2)}) %all-to-all-start.2) | async-done | bytes 786464 | tf_op jit(solution)/shard_map/all_to_all | solution.py:89
  172.7 5.5 all-to-all-start.4
  187.1 9.8 %all-to-all-done.4 = bf16[16,32,768]{2,1,0:T(8,128)(2,1)} async-done(((bf16[16,32,768]{2,1,0:T(8,128)(2,1)}), bf16[16,32,768]{2,1,0:T(8,128)(2,1)}, u32[]{:S(2)}, u32[]{:S(2)}) %all-to-all-start.4) | async-done | bytes 786464 | tf_op jit(solution)/shard_map/all_to_all | solution.py:89
  197.0 5.5 all-to-all-start.10
  205.6 8.0 %constant_dynamic-update-slice_fusion.11 = (bf16[3072,3072]{1,0:T(8,128)(2,1)}, bf16[512,3072]{1,0:T(8,128)(2,1)}, f32[512,3072]{1,0:T(8,128)}) fusion(bf16[512,768]{1,0:T(8,128)(2,1)} %bitcast.15, bf16[1,768,3072]{2,1,0:T(8,128)(2,1)} %param.16), kind=kOutput, calls=%fused_computation.379 | convolution fusion | flops 2423783424 | bytes 18087936 | tf_op jit(solution)/shard_map/dot_general | solution.py:21
  218.8 2.5 all-to-all-done.10
  221.3 14.1 %collective-permute-done.1 = bf16[512,768]{1,0:T(8,128)(2,1)} collective-permute-done((bf16[512,768]{1,0:T(8,128)(2,1)}, bf16[512,768]{1,0:T(8,128)(2,1)}, u32[]{:S(2)}, u32[]{:S(2)}) %collective-permute-start.1) | collective-permute-done | bytes 786464 | tf_op jit(solution)/shard_map/ppermute | solution.py:168
  238.4 13.8 %collective-permute-done = bf16[512,768]{1,0:T(8,128)(2,1)} collective-permute-done((bf16[512,768]{1,0:T(8,128)(2,1)}, bf16[512,768]{1,0:T(8,128)(2,1)}, u32[]{:S(2)}, u32[]{:S(2)}) %collective-permute-start) | collective-permute-done | bytes 786464 | tf_op jit(solution)/shard_map/ppermute | solution.py:168
  253.7 15.3 %collective-permute-done.2 = bf16[512,768]{1,0:T(8,128)(2,1)} collective-permute-done((bf16[512,768]{1,0:T(8,128)(2,1)}, bf16[512,768]{1,0:T(8,128)(2,1)}, u32[]{:S(2)}, u32[]{:S(2)}) %collective-permute-start.2) | collective-permute-done | bytes 786464 | tf_op jit(solution)/shard_map/ppermute | solution.py:168
  276.3 11.2 %constant_dynamic-update-slice_fusion.8 = (bf16[3072,3072]{1,0:T(8,128)(2,1)}, bf16[512,3072]{1,0:T(8,128)(2,1)}) fusion(f32[512,3072]{1,0:T(8,128)} %get-tuple-element.115, bf16[512,768]{1,0:T(8,128)(2,1)S(1)} %bitcast.483, bf16[1,3072,768]{2,1,0:T(8,128)(2,1)} %param.17), kind=kOutput, calls=%fused_computation.376 | convolution fusion | flops 2431647744 | bytes 18087936 | tf_op jit(solution)/shard_map/dot_general | solution.py:17
  287.5 6.9 %fusion.77 = (bf16[3072,3072]{1,0:T(8,128)(2,1)}, f32[512,3072]{1,0:T(8,128)}) fusion(bf16[3072,3072]{1,0:T(8,128)(2,1)} %get-tuple-element.78, bf16[512,768]{1,0:T(8,128)(2,1)} %collective-permute-done, bf16[1,768,3072]{2,1,0:T(8,128)(2,1)S(1)} %bitcast.494), kind=kOutput, calls=%fused_computation.96 | convolution fusion | flops 2423783424 | bytes 14942208 | tf_op jit(solution)/shard_map/dot_general | solution.py:21
  300.2 6.3 constant_dynamic-update-slice_fusion.10
  306.5 8.2 %fusion.74 = bf16[3072,3072]{1,0:T(8,128)(2,1)} fusion(bf16[3072,3072]{1,0:T(8,128)(2,1)} %get-tuple-element.149, f32[512,3072]{1,0:T(8,128)} %get-tuple-element.117, bf16[1,3072,768]{2,1,0:T(8,128)(2,1)} %param.17, bf16[512,768]{1,0:T(8,128)(2,1)} %collective-permute-done.3, f32[512]{0:T(512)S(1)} %copy-done.103), kind=kOutput, calls=%fused_computation.92 | convolution fusion | flops 2432827392 | bytes 14944256 | tf_op jit(solution)/shard_map/dot_general | solution.py:17
  314.7 5.7 constant_dynamic-update-slice_fusion.7
  320.4 6.1 fusion.78
  330.1 4.6 fusion.90
  337.5 5.7 constant_dynamic-update-slice_fusion.9
  343.2 5.7 fusion.71
  348.9 5.2 constant_dynamic-update-slice_fusion.6
  354.1 2.6 fusion.56
  356.8 4.6 fusion.92
  361.4 2.4 add_convert_fusion
  363.8 6.2 all-to-all-start.11
  370.0 7.1 %fusion.88 = (f32[512]{0:T(512)S(1)}, bf16[512,768]{1,0:T(8,128)(2,1)}) fusion(bf16[16,32,768]{2,1,0:T(8,128)(2,1)} %all-to-all-done.6, f32[512]{0:T(512)} %get-tuple-element.73, bf16[512,3072]{1,0:T(8,128)(2,1)} %get-tuple-element.79, bf16[1,3072,768]{2,1,0:T(8,128)(2,1)} %param.17), kind=kOutput, calls=%fused_computation.128 | convolution fusion | flops 2417884672 | bytes 9441280 | tf_op jit(solution)/shard_map/dot_general | solution.py:21
  377.2 5.1 fusion.60
  382.4 2.4 fusion.207
  389.1 2.3 add_convert_fusion.2
  391.4 3.8 fusion.58
  395.2 6.1 all-to-all-start.7
  405.8 2.3 add_convert_fusion.1
  408.1 7.0 %fusion.79 = (bf16[3072,3072]{1,0:T(8,128)(2,1)}, f32[512,3072]{1,0:T(8,128)}) fusion(bf16[3072,3072]{1,0:T(8,128)(2,1)} %get-tuple-element.74, bf16[512,768]{1,0:T(8,128)(2,1)} %collective-permute-done.2, bf16[1,768,3072]{2,1,0:T(8,128)(2,1)} %param.16), kind=kOutput, calls=%fused_computation.98 | convolution fusion | flops 2423783424 | bytes 14942208 | tf_op jit(solution)/shard_map/dot_general | solution.py:21
  415.1 5.0 all-to-all-done.7
  420.1 5.5 all-to-all-start.9
  429.5 3.6 multiply_reduce_fusion.8
  433.1 11.3 %all-to-all-done.9 = bf16[16,32,768]{2,1,0:T(8,128)(2,1)} async-done(((bf16[16,32,768]{2,1,0:T(8,128)(2,1)}), bf16[16,32,768]{2,1,0:T(8,128)(2,1)}, u32[]{:S(2)}, u32[]{:S(2)}) %all-to-all-start.9) | async-done | bytes 786464 | tf_op jit(solution)/shard_map/all_to_all | solution.py:89
  444.4 5.5 all-to-all-start.5
  450.2 4.8 fusion.272
  455.8 2.6 convolution_convert_fusion.17
  470.0 2.5 convolution_convert_fusion.18
  481.3 2.5 convolution_convert_fusion.19
  493.1 6.5 convolution_convert_fusion
  502.3 2.5 fusion.175
  505.2 4.9 fusion.37
  510.1 21.7 %convolution_bitcast_fusion.1 = f32[1,3072,768]{2,1,0:T(8,128)} fusion(bf16[3072,3072]{1,0:T(8,128)(2,1)} %get-tuple-element.155, bf16[3072,768]{1,0:T(8,128)(2,1)} %fusion.208), kind=kOutput, calls=%fused_computation.57 | convolution fusion | flops 14495514624 | bytes 33030144 | tf_op jit(solution)/shard_map/dot_general | solution.py:13
  540.2 2.3 constant_dynamic-update-slice_fusion
  542.5 8.3 %fusion.68 = bf16[3072,3072]{1,0:T(8,128)(2,1)} fusion(bf16[3072,3072]{1,0:T(8,128)(2,1)} %get-tuple-element.153, f32[512,3072]{1,0:T(8,128)} %get-tuple-element.156, bf16[1,3072,768]{2,1,0:T(8,128)(2,1)} %param.17, bf16[512,768]{1,0:T(8,128)(2,1)} %collective-permute-done.5, f32[512]{0:T(512)S(1)} %copy-done.100), kind=kOutput, calls=%fused_computation.90 | convolution fusion | flops 2432827392 | bytes 14944256 | tf_op jit(solution)/shard_map/dot_general | solution.py:17
  550.8 6.0 all-to-all-start.3
  556.8 21.5 %convolution_bitcast_fusion = f32[1,768,3072]{2,1,0:T(8,128)} fusion(bf16[3072,768]{1,0:T(8,128)(2,1)} %constant_dynamic-update-slice_fusion, bf16[3072,3072]{1,0:T(8,128)(2,1)} %fusion.68), kind=kOutput, calls=%fused_computation.56 | convolution fusion | flops 14495514624 | bytes 33030144 | tf_op jit(solution)/shard_map/dot_general | solution.py:13
  578.2 3.9 all-to-all-done.3
  582.1 6.6 %all-to-all-start.1 = ((bf16[16,32,768]{2,1,0:T(8,128)(2,1)}), bf16[16,32,768]{2,1,0:T(8,128)(2,1)}, u32[]{:S(2)}, u32[]{:S(2)}) async-start(bf16[16,32,768]{2,1,0:T(8,128)(2,1)} %bitcast.478), calls=%async_computation.1 | async-start | bytes 1572864 | tf_op jit(solution)/shard_map/all_to_all | solution.py:89
  595.4 16.5 %reduce-scatter.2.cloned.1.call-done = bf16[48,3200]{1,0:T(8,128)(2,1)} async-done(((bf16[768,3200]{1,0:T(8,128)(2,1)}), bf16[48,3200]{1,0:T(8,128)(2,1)}) %reduce-scatter.2.cloned.1.call-update) | async-done | bytes 307216 | tf_op jit(solution)/shard_map/reduce_scatter | solution.py:208
  615.8 21.2 %all-reduce.4.cloned.1.call-done = bf16[48,3200]{1,0:T(8,128)(2,1)} async-done(((bf16[48,3200]{1,0:T(8,128)(2,1)}), bf16[48,3200]{1,0:T(8,128)(2,1)}) %all-reduce.4.cloned.1.call-update) | async-done | bytes 307216 | tf_op jit(solution)/shard_map/psum | solution.py:209
  (407 shorter events, 147.2 us)
Async XLA Ops:
  7.2 13.9 %copy-start.7 = (bf16[3,1,197,768]{3,2,1,0:T(8,128)(2,1)S(1)}, bf16[3,1,197,768]{3,2,1,0:T(8,128)(2,1)}, u32[]{:S(2)}) copy-start(bf16[3,1,197,768]{3,2,1,0:T(8,128)(2,1)} %param.10) | copy-start | bytes 2723332
  7.2 72.9 %all-gather.2.cloned.1.call-start = ((), (), s32[]{:S(2)}) async-start(), calls=%async_computation.13 | async-start | bytes 5222400 | tf_op jit(solution)/shard_map/all_gather | solution.py:126
  13.7 87.3 %all-to-all-start.6 = ((bf16[16,32,768]{2,1,0:T(8,128)(2,1)}), bf16[16,32,768]{2,1,0:T(8,128)(2,1)}, u32[]{:S(2)}, u32[]{:S(2)}) async-start(bf16[16,32,768]{2,1,0:T(8,128)(2,1)} %bitcast.48), calls=%async_computation.6 | async-start | bytes 1572864 | tf_op jit(solution)/shard_map/all_to_all | solution.py:89
  21.3 64.3 %copy-start.82 = (f32[197]{0:T(256)}, f32[197]{0:T(256)S(1)}, u32[]{:S(2)}) copy-start(f32[197]{0:T(256)S(1)} %broadcast_multiply_fusion.17) | copy-start | bytes 2368
  21.3 64.3 %copy-start.80 = (f32[197]{0:T(256)}, f32[197]{0:T(256)S(1)}, u32[]{:S(2)}) copy-start(f32[197]{0:T(256)S(1)} %get-tuple-element.158) | copy-start | bytes 2368
  21.4 64.3 %copy-start.88 = (f32[197]{0:T(256)}, f32[197]{0:T(256)S(1)}, u32[]{:S(2)}) copy-start(f32[197]{0:T(256)S(1)} %get-tuple-element.157) | copy-start | bytes 2368
  21.8 63.9 %copy-start.92 = (f32[197]{0:T(256)}, f32[197]{0:T(256)S(1)}, u32[]{:S(2)}) copy-start(f32[197]{0:T(256)S(1)} %add_rsqrt_fusion.1) | copy-start | bytes 2368
  21.8 63.9 %copy-start.90 = (f32[197]{0:T(256)}, f32[197]{0:T(256)S(1)}, u32[]{:S(2)}) copy-start(f32[197]{0:T(256)S(1)} %add_rsqrt_fusion.3) | copy-start | bytes 2368
  21.9 63.8 %copy-start.94 = (f32[197]{0:T(256)}, f32[197]{0:T(256)S(1)}, u32[]{:S(2)}) copy-start(f32[197]{0:T(256)S(1)} %add_rsqrt_fusion.5) | copy-start | bytes 2368
  100.9 8.6 %copy-start.2 = (f32[12,197,197]{1,2,0:T(8,128)}, f32[12,197,197]{1,2,0:T(8,128)S(1)}, u32[]{:S(2)}) copy-start(f32[12,197,197]{1,2,0:T(8,128)S(1)} %get-tuple-element.119) | copy-start | bytes 5588500
  100.9 23.0 %all-to-all-start.8 = ((bf16[16,32,768]{2,1,0:T(8,128)(2,1)}), bf16[16,32,768]{2,1,0:T(8,128)(2,1)}, u32[]{:S(2)}, u32[]{:S(2)}) async-start(bf16[16,32,768]{2,1,0:T(8,128)(2,1)} %bitcast.463), calls=%async_computation.8 | async-start | bytes 1572864 | tf_op jit(solution)/shard_map/all_to_all | solution.py:89
  109.5 20.1 %copy-start.41 = (bf16[12,64,197]{2,1,0:T(8,128)(2,1)S(1)}, bf16[12,64,197]{2,1,0:T(8,128)(2,1)}, u32[]{:S(2)}) copy-start(bf16[12,64,197]{2,1,0:T(8,128)(2,1)} %convolution_convert_fusion.15) | copy-start | bytes 907780
  123.9 24.4 %all-to-all-start = ((bf16[16,32,768]{2,1,0:T(8,128)(2,1)}), bf16[16,32,768]{2,1,0:T(8,128)(2,1)}, u32[]{:S(2)}, u32[]{:S(2)}) async-start(bf16[16,32,768]{2,1,0:T(8,128)(2,1)} %bitcast.14), calls=%async_computation | async-start | bytes 1572864 | tf_op jit(solution)/shard_map/all_to_all | solution.py:89
  134.8 327.4 %copy-start.5 = (f32[12,197,197]{1,2,0:T(8,128)}, f32[12,197,197]{1,2,0:T(8,128)S(1)}, u32[]{:S(2)}) copy-start(f32[12,197,197]{1,2,0:T(8,128)S(1)} %get-tuple-element.110) | copy-start | bytes 5588500
  148.4 24.3 %all-to-all-start.2 = ((bf16[16,32,768]{2,1,0:T(8,128)(2,1)}), bf16[16,32,768]{2,1,0:T(8,128)(2,1)}, u32[]{:S(2)}, u32[]{:S(2)}) async-start(bf16[16,32,768]{2,1,0:T(8,128)(2,1)} %bitcast.466), calls=%async_computation.2 | async-start | bytes 1572864 | tf_op jit(solution)/shard_map/all_to_all | solution.py:89
  158.2 38.8 %copy-start.86 = (f32[197]{0:T(256)}, f32[197]{0:T(256)S(1)}, u32[]{:S(2)}) copy-start(f32[197]{0:T(256)S(1)} %broadcast_multiply_fusion.12) | copy-start | bytes 2368
  158.9 38.0 %copy-start.98 = (f32[197]{0:T(256)}, f32[197]{0:T(256)S(1)}, u32[]{:S(2)}) copy-start(f32[197]{0:T(256)S(1)} %add_rsqrt_fusion) | copy-start | bytes 2368
  172.7 24.3 %all-to-all-start.4 = ((bf16[16,32,768]{2,1,0:T(8,128)(2,1)}), bf16[16,32,768]{2,1,0:T(8,128)(2,1)}, u32[]{:S(2)}, u32[]{:S(2)}) async-start(bf16[16,32,768]{2,1,0:T(8,128)(2,1)} %bitcast.465), calls=%async_computation.4 | async-start | bytes 1572864 | tf_op jit(solution)/shard_map/all_to_all | solution.py:89
  181.0 125.5 %collective-permute-start.3 = (bf16[512,768]{1,0:T(8,128)(2,1)}, bf16[512,768]{1,0:T(8,128)(2,1)}, u32[]{:S(2)}, u32[]{:S(2)}) collective-permute-start(bf16[512,768]{1,0:T(8,128)(2,1)} %bitcast.50), channel_id=1, source_target_pairs={{0,16},{16,0},{1,17},{17,1},{2,18},{18,2},{3,19},{19,3},{4,20},{20... | collective-permute-start | bytes 2359304 | tf_op jit(solution)/shard_map/ppermute | solution.py:168
  182.4 160.8 %collective-permute-start.4 = (bf16[512,768]{1,0:T(8,128)(2,1)}, bf16[512,768]{1,0:T(8,128)(2,1)}, u32[]{:S(2)}, u32[]{:S(2)}) collective-permute-start(bf16[512,768]{1,0:T(8,128)(2,1)} %bitcast.65), channel_id=1, source_target_pairs={{0,16},{16,0},{1,17},{17,1},{2,18},{18,2},{3,19},{19,3},{4,20},{20... | collective-permute-start | bytes 2359304 | tf_op jit(solution)/shard_map/ppermute | solution.py:168
  183.0 52.4 %collective-permute-start.1 = (bf16[512,768]{1,0:T(8,128)(2,1)}, bf16[512,768]{1,0:T(8,128)(2,1)}, u32[]{:S(2)}, u32[]{:S(2)}) collective-permute-start(bf16[512,768]{1,0:T(8,128)(2,1)} %bitcast.30), channel_id=1, source_target_pairs={{0,16},{16,0},{1,17},{17,1},{2,18},{18,2},{3,19},{19,3},{4,20},{20... | collective-permute-start | bytes 2359304 | tf_op jit(solution)/shard_map/ppermute | solution.py:168
  184.5 67.7 %collective-permute-start = (bf16[512,768]{1,0:T(8,128)(2,1)}, bf16[512,768]{1,0:T(8,128)(2,1)}, u32[]{:S(2)}, u32[]{:S(2)}) collective-permute-start(bf16[512,768]{1,0:T(8,128)(2,1)} %bitcast.15), channel_id=1, source_target_pairs={{0,16},{16,0},{1,17},{17,1},{2,18},{18,2},{3,19},{19,3},{4,20},{20... | collective-permute-start | bytes 2359304 | tf_op jit(solution)/shard_map/ppermute | solution.py:168
  197.0 24.3 %all-to-all-start.10 = ((bf16[16,32,768]{2,1,0:T(8,128)(2,1)}), bf16[16,32,768]{2,1,0:T(8,128)(2,1)}, u32[]{:S(2)}, u32[]{:S(2)}) async-start(bf16[16,32,768]{2,1,0:T(8,128)(2,1)} %bitcast.464), calls=%async_computation.10 | async-start | bytes 1572864 | tf_op jit(solution)/shard_map/all_to_all | solution.py:89
  202.5 66.6 %collective-permute-start.2 = (bf16[512,768]{1,0:T(8,128)(2,1)}, bf16[512,768]{1,0:T(8,128)(2,1)}, u32[]{:S(2)}, u32[]{:S(2)}) collective-permute-start(bf16[512,768]{1,0:T(8,128)(2,1)} %bitcast.43), channel_id=1, source_target_pairs={{0,16},{16,0},{1,17},{17,1},{2,18},{18,2},{3,19},{19,3},{4,20},{20... | collective-permute-start | bytes 2359304 | tf_op jit(solution)/shard_map/ppermute | solution.py:168
  205.5 8.0 %copy-start.30 = (f32[512,16]{0,1:T(8,128)}, f32[512,16]{0,1:T(8,128)S(1)}, u32[]{:S(2)}) copy-start(f32[512,16]{0,1:T(8,128)S(1)} %get-tuple-element.139) | copy-start | bytes 98308
  205.5 8.0 %copy-start.60 = (f32[512]{0:T(512)}, f32[512]{0:T(512)S(1)}, u32[]{:S(2)}) copy-start(f32[512]{0:T(512)S(1)} %get-tuple-element.138) | copy-start | bytes 6148
  235.3 168.2 %collective-permute-start.5 = (bf16[512,768]{1,0:T(8,128)(2,1)}, bf16[512,768]{1,0:T(8,128)(2,1)}, u32[]{:S(2)}, u32[]{:S(2)}) collective-permute-start(bf16[512,768]{1,0:T(8,128)(2,1)} %bitcast.80), channel_id=1, source_target_pairs={{0,16},{16,0},{1,17},{17,1},{2,18},{18,2},{3,19},{19,3},{4,20},{20... | collective-permute-start | bytes 2359304 | tf_op jit(solution)/shard_map/ppermute | solution.py:168
  274.8 12.7 %slice-start.2 = ((s8[4718592]{0:T(1024)(128)(4,1)}), s8[4194304]{0:T(1024)(128)(4,1)S(1)}, s32[]{:S(2)}) async-start(s8[4718592]{0:T(1024)(128)(4,1)} %bitcast.493), calls=%async_computation.18 | async-start | bytes 8388608
  276.3 11.2 %slice-start.3 = ((s8[4718592]{0:T(1024)(128)(4,1)}), s8[524288]{0:T(1024)(128)(4,1)S(1)}, s32[]{:S(2)}) async-start(s8[4718592]{0:T(1024)(128)(4,1)} %bitcast.493), calls=%async_computation.19 | async-start | bytes 1048576
  287.5 9.1 %copy-start.67 = (f32[512]{0:T(512)S(1)}, f32[512]{0:T(512)}, u32[]{:S(2)}) copy-start(f32[512]{0:T(512)} %get-tuple-element.73) | copy-start | bytes 6148
  300.2 14.5 %slice-start.8 = ((s8[4718592]{0:T(1024)(128)(4,1)}), s8[4194304]{0:T(1024)(128)(4,1)S(1)}, s32[]{:S(2)}) async-start(s8[4718592]{0:T(1024)(128)(4,1)} %bitcast.499), calls=%async_computation.24 | async-start | bytes 8388608
  306.5 8.2 %copy-start.32 = (bf16[16,32,768]{2,1,0:T(8,128)(2,1)S(1)}, bf16[16,32,768]{2,1,0:T(8,128)(2,1)}, u32[]{:S(2)}) copy-start(bf16[16,32,768]{2,1,0:T(8,128)(2,1)} %multiply_convert_fusion.13) | copy-start | bytes 2359300
  306.5 8.2 %slice-start.9 = ((s8[4718592]{0:T(1024)(128)(4,1)}), s8[524288]{0:T(1024)(128)(4,1)S(1)}, s32[]{:S(2)}) async-start(s8[4718592]{0:T(1024)(128)(4,1)} %bitcast.499), calls=%async_computation.25 | async-start | bytes 1048576
  306.5 13.9 %slice-start.4 = ((s8[4718592]{0:T(1024)(128)(4,1)}), s8[4194304]{0:T(1024)(128)(4,1)S(1)}, s32[]{:S(2)}) async-start(s8[4718592]{0:T(1024)(128)(4,1)} %bitcast.495), calls=%async_computation.20 | async-start | bytes 8388608
  320.4 9.7 %copy-start.69 = (f32[512]{0:T(512)S(1)}, f32[512]{0:T(512)}, u32[]{:S(2)}) copy-start(f32[512]{0:T(512)} %get-tuple-element.69) | copy-start | bytes 6148
  363.8 31.4 %all-to-all-start.11 = ((bf16[16,32,768]{2,1,0:T(8,128)(2,1)}), bf16[16,32,768]{2,1,0:T(8,128)(2,1)}, u32[]{:S(2)}, u32[]{:S(2)}) async-start(bf16[16,32,768]{2,1,0:T(8,128)(2,1)} %bitcast.469), calls=%async_computation.11 | async-start | bytes 1572864 | tf_op jit(solution)/shard_map/all_to_all | solution.py:89
  377.1 14.2 %slice-start.6 = ((s8[4718592]{0:T(1024)(128)(4,1)}), s8[4194304]{0:T(1024)(128)(4,1)S(1)}, s32[]{:S(2)}) async-start(s8[4718592]{0:T(1024)(128)(4,1)} %bitcast.497), calls=%async_computation.22 | async-start | bytes 8388608
  377.2 7.6 %copy-start.31 = (f32[512,16]{0,1:T(8,128)S(1)}, f32[512,16]{0,1:T(8,128)}, u32[]{:S(2)}) copy-start(f32[512,16]{0,1:T(8,128)} %copy-done.30) | copy-start | bytes 98308
  377.2 7.6 %copy-start.61 = (f32[512]{0:T(512)S(1)}, f32[512]{0:T(512)}, u32[]{:S(2)}) copy-start(f32[512]{0:T(512)} %copy-done.60) | copy-start | bytes 6148
  377.2 7.6 %copy-start.64 = (f32[512]{0:T(512)S(1)}, f32[512]{0:T(512)}, u32[]{:S(2)}) copy-start(f32[512]{0:T(512)} %fusion.240) | copy-start | bytes 6148
  377.2 9.6 %copy-start.66 = (f32[512]{0:T(512)S(1)}, f32[512]{0:T(512)}, u32[]{:S(2)}) copy-start(f32[512]{0:T(512)} %get-tuple-element.70) | copy-start | bytes 6148
  377.2 14.1 %slice-start.7 = ((s8[4718592]{0:T(1024)(128)(4,1)}), s8[524288]{0:T(1024)(128)(4,1)S(1)}, s32[]{:S(2)}) async-start(s8[4718592]{0:T(1024)(128)(4,1)} %bitcast.497), calls=%async_computation.23 | async-start | bytes 1048576
  382.4 9.0 %copy-start.109 = (bf16[512,3072]{1,0:T(8,128)(2,1)S(1)}, bf16[512,3072]{1,0:T(8,128)(2,1)}, u32[]{:S(2)}) copy-start(bf16[512,3072]{1,0:T(8,128)(2,1)} %get-tuple-element.152) | copy-start | bytes 9437188
  395.2 24.9 %all-to-all-start.7 = ((bf16[16,32,768]{2,1,0:T(8,128)(2,1)}), bf16[16,32,768]{2,1,0:T(8,128)(2,1)}, u32[]{:S(2)}, u32[]{:S(2)}) async-start(bf16[16,32,768]{2,1,0:T(8,128)(2,1)} %bitcast.468), calls=%async_computation.7 | async-start | bytes 1572864 | tf_op jit(solution)/shard_map/all_to_all | solution.py:89
  408.1 17.5 %copy-start.63 = (f32[512]{0:T(512)S(1)}, f32[512]{0:T(512)}, u32[]{:S(2)}) copy-start(f32[512]{0:T(512)} %fusion.244) | copy-start | bytes 6148
  408.1 17.6 %copy-start.76 = (f32[16]{0:T(128)S(1)}, f32[16]{0:T(128)}, u32[]{:S(2)}) copy-start(f32[16]{0:T(128)} %compare_convert_fusion) | copy-start | bytes 196
  420.1 24.3 %all-to-all-start.9 = ((bf16[16,32,768]{2,1,0:T(8,128)(2,1)}), bf16[16,32,768]{2,1,0:T(8,128)(2,1)}, u32[]{:S(2)}, u32[]{:S(2)}) async-start(bf16[16,32,768]{2,1,0:T(8,128)(2,1)} %bitcast.467), calls=%async_computation.9 | async-start | bytes 1572864 | tf_op jit(solution)/shard_map/all_to_all | solution.py:89
  427.0 23.2 %copy-start.73 = (f32[197]{0:T(256)S(1)}, f32[197]{0:T(256)}, u32[]{:S(2)}) copy-start(f32[197]{0:T(256)} %copy-done.72) | copy-start | bytes 2368
  427.0 23.2 %copy-start.79 = (f32[197]{0:T(256)S(1)}, f32[197]{0:T(256)}, u32[]{:S(2)}) copy-start(f32[197]{0:T(256)} %copy-done.78) | copy-start | bytes 2368
  427.0 23.2 %copy-start.85 = (f32[197]{0:T(256)S(1)}, f32[197]{0:T(256)}, u32[]{:S(2)}) copy-start(f32[197]{0:T(256)} %copy-done.84) | copy-start | bytes 2368
  427.1 23.2 %copy-start.87 = (f32[197]{0:T(256)S(1)}, f32[197]{0:T(256)}, u32[]{:S(2)}) copy-start(f32[197]{0:T(256)} %copy-done.86) | copy-start | bytes 2368
  427.1 23.2 %copy-start.97 = (f32[197]{0:T(256)S(1)}, f32[197]{0:T(256)}, u32[]{:S(2)}) copy-start(f32[197]{0:T(256)} %copy-done.96) | copy-start | bytes 2368
  427.1 23.2 %copy-start.99 = (f32[197]{0:T(256)S(1)}, f32[197]{0:T(256)}, u32[]{:S(2)}) copy-start(f32[197]{0:T(256)} %copy-done.98) | copy-start | bytes 2368
  444.4 106.4 %all-to-all-start.5 = ((bf16[16,32,768]{2,1,0:T(8,128)(2,1)}), bf16[16,32,768]{2,1,0:T(8,128)(2,1)}, u32[]{:S(2)}, u32[]{:S(2)}) async-start(bf16[16,32,768]{2,1,0:T(8,128)(2,1)} %bitcast.480), calls=%async_computation.5 | async-start | bytes 1572864 | tf_op jit(solution)/shard_map/all_to_all | solution.py:89
  449.9 162.0 %reduce-scatter.2.cloned.1.call-start = ((), (), s32[]{:S(2)}) async-start(), calls=%async_computation.14 | async-start | bytes 5222400 | tf_op jit(solution)/shard_map/reduce_scatter | solution.py:208
  465.8 8.6 %copy-start.3 = (f32[12,197,197]{1,2,0:T(8,128)S(1)}, f32[12,197,197]{1,2,0:T(8,128)}, u32[]{:S(2)}) copy-start(f32[12,197,197]{1,2,0:T(8,128)} %copy-done.2) | copy-start | bytes 5588500
  465.8 8.6 %copy-start.38 = (f32[12,197]{1,0:T(8,128)S(1)}, f32[12,197]{1,0:T(8,128)}, u32[]{:S(2)}) copy-start(f32[12,197]{1,0:T(8,128)} %copy-done.37) | copy-start | bytes 28372
  491.9 7.7 %slice-start = ((s8[4915200]{0:T(1024)(128)(4,1)}), s8[4194304]{0:T(1024)(128)(4,1)S(1)}, s32[]{:S(2)}) async-start(s8[4915200]{0:T(1024)(128)(4,1)} %bitcast.476), calls=%async_computation.16 | async-start | bytes 8388608
  533.9 8.5 %copy-start.100 = (f32[512]{0:T(512)S(1)}, f32[512]{0:T(512)}, u32[]{:S(2)}) copy-start(f32[512]{0:T(512)} %get-tuple-element.68) | copy-start | bytes 6148
  550.8 31.4 %all-to-all-start.3 = ((bf16[16,32,768]{2,1,0:T(8,128)(2,1)}), bf16[16,32,768]{2,1,0:T(8,128)(2,1)S(1)}, u32[]{:S(2)}, u32[]{:S(2)}) async-start(bf16[16,32,768]{2,1,0:T(8,128)(2,1)} %bitcast.479), calls=%async_computation.3 | async-start | bytes 1572864 | tf_op jit(solution)/shard_map/all_to_all | solution.py:89
  556.7 32.1 %copy-start.20 = (f32[197,768]{1,0:T(8,128)S(1)}, f32[197,768]{1,0:T(8,128)}, u32[]{:S(2)}) copy-start(f32[197,768]{1,0:T(8,128)} %get-tuple-element.83) | copy-start | bytes 1815556
  582.1 31.1 %all-to-all-start.1 = ((bf16[16,32,768]{2,1,0:T(8,128)(2,1)}), bf16[16,32,768]{2,1,0:T(8,128)(2,1)}, u32[]{:S(2)}, u32[]{:S(2)}) async-start(bf16[16,32,768]{2,1,0:T(8,128)(2,1)} %bitcast.478), calls=%async_computation.1 | async-start | bytes 1572864 | tf_op jit(solution)/shard_map/all_to_all | solution.py:89
  588.7 48.3 %all-reduce.4.cloned.1.call-start = ((), (), s32[]{:S(2)}) async-start(), calls=%async_computation.15 | async-start | bytes 614400 | tf_op jit(solution)/shard_map/psum | solution.py:209
  592.4 20.9 %copy-start.14 = (f32[197,768]{1,0:T(8,128)S(1)}, f32[197,768]{1,0:T(8,128)}, u32[]{:S(2)}) copy-start(f32[197,768]{1,0:T(8,128)} %copy-done.13) | copy-start | bytes 1815556
  (77 other events, 238.9 us)
Sparse Core Ops, SparseCore 0:
  10.8 69.3 all-gather.1
  510.2 101.5 reduce-scatter.1
  614.3 22.7 all-reduce.3
